TPU v7x, 256 devices: a whole 4x4x8 slice. The times are simulated.
256 devices in a mesh: dp: 8 (over y, z_hi), mp: 32 (over z_lo, x, core).
Axes of the slice: x: 4, y: 4, z: 8 (z_hi: 2, z_lo: 4; z = z_hi * 4 + z_lo), core: 2. Of those that a mesh axis runs over, the one named last changes fastest.
Arguments:
- tokens: bfloat16 [131072, 4096], P(('dp', 'mp')), may hold values from -170 to 170
- outgrads: bfloat16 [131072, 4096], P(('dp', 'mp')), may hold values from -11 to 11
- grad_parts: bfloat16 [8, 64, 512, 512], P('dp', 'mp'), may hold values from -6 to 6
- basis_slots: bfloat16 [32, 512, 512], P('mp'), may hold values from -0.25 to 0.25
- pattern: int32 [2, 8], replicated, may hold values from 0 to 7, each once within a row
- owners: int32 [16], replicated, may hold values from 0 to 31, as said below
Outputs:
- precond: bfloat16 [64, 512, 512], P('mp')
- eigenvalues: float32 [16, 512], replicated
Inputs may be any that keep to these rules, and one draw needn't show every extreme that they name: `pattern`: each row is a permutation of 0 to 7. `owners`: the entries are distinct; 0 and 31 are always among them.
All inputs are finite; a program needn't handle non-finite values.
Results may differ from a plain program's by a relative error of at most 0.006.
Values may be sent and summed in bfloat16 or wider, within the bound.
A program may use at most 128 MiB of HBM per device.

v0:
```python
import jax
import jax.numpy as jnp
from jax import lax
from jax.sharding import PartitionSpec as P

DAMPING = 0.5


def inverse_order(placing):
    places = jnp.arange(placing.shape[0], dtype=jnp.int32)
    hits = (placing[:, None] == places[None, :]).astype(jnp.int32)
    return jnp.sum(places[:, None] * hits, axis=0)


def side_moments(values, placing, side_bases):
    blocks = values.reshape(values.shape[0], placing.shape[0], -1)
    selected = jnp.take(blocks, placing, axis=1)
    projected = jnp.einsum("tbi,bij->tbj", selected, side_bases, preferred_element_type=jnp.float32)
    return jnp.sum(projected * projected, axis=0)


def precondition(gradient, out_basis, in_basis, out_scale, in_scale):
    contract = (((0,), (0,)), ((), ()))
    halfway = lax.dot_general(
        out_basis, gradient, contract, preferred_element_type=jnp.float32
    ).astype(jnp.bfloat16)
    rotated = jnp.dot(halfway, in_basis, preferred_element_type=jnp.float32)
    scaled = (rotated / (out_scale[:, None] * in_scale[None, :] + DAMPING)).astype(jnp.bfloat16)
    returned = jnp.dot(out_basis, scaled, preferred_element_type=jnp.float32).astype(jnp.bfloat16)
    trailing = (((1,), (1,)), ((), ()))
    return lax.dot_general(returned, in_basis, trailing, preferred_element_type=jnp.float32).astype(
        jnp.bfloat16
    )


def local(tokens, outgrads, grad_parts, basis_slots, pattern, owners):
    summed = lax.psum(grad_parts[0].astype(jnp.float32), "dp").astype(jnp.bfloat16)
    gathered = lax.all_gather(basis_slots, "mp", axis=0, tiled=True)
    picked = jnp.take(gathered, owners, axis=0)
    blocks_per_side = pattern.shape[1]
    block_width = basis_slots.shape[1]
    bases_used = picked.reshape(2, blocks_per_side, block_width, block_width)
    moments = jnp.stack(
        [
            side_moments(outgrads, pattern[0], bases_used[0]),
            side_moments(tokens, pattern[1], bases_used[1]),
        ]
    )
    token_count = tokens.shape[0] * lax.axis_size("dp") * lax.axis_size("mp")
    eigenvalues = lax.psum(moments, ("dp", "mp")) / token_count
    out_inverse = inverse_order(pattern[0])
    in_inverse = inverse_order(pattern[1])
    leading = lax.axis_index("mp") * summed.shape[0]
    results = []
    for offset in range(summed.shape[0]):
        number = leading + offset
        out_place = out_inverse[number // blocks_per_side]
        in_place = in_inverse[number % blocks_per_side]
        results.append(
            precondition(
                summed[offset],
                bases_used[0, out_place],
                bases_used[1, in_place],
                eigenvalues[0, out_place],
                eigenvalues[1, in_place],
            )
        )
    precond = jnp.stack(results)
    return (precond, eigenvalues.reshape(2 * blocks_per_side, block_width))


def solution(mesh):
    placed = (
        P(("dp", "mp"), None),
        P(("dp", "mp"), None),
        P("dp", "mp", None, None),
        P("mp", None, None),
        P(),
        P(),
    )
    return jax.shard_map(
        local, mesh=mesh, in_specs=placed, out_specs=(P("mp", None, None), P()), check_vma=False
    )
```

profile of v0, /device:TPU:1, one launch (start us, length us, event | category | flops | bytes accessed | tf_op | source)
XLA Modules:
  0.0 416.0 jit_solution(15169400836273239119)
XLA Ops:
  7.2 0.0 all-gather.2.cloned.1.call-start
  7.2 0.7 all-gather.2.cloned.1.call-update
  7.9 0.8 slice_bitcast_fusion.7
  8.7 0.1 select_reduce_fusion
  8.8 0.7 fusion.54
  12.0 0.6 fusion.53
  15.2 0.7 compare_and_fusion.2
  15.9 0.1 broadcast_in_dim.31
  16.0 1.5 bitcast_convert_fusion
  17.5 6.5 %copy.18 = bf16[512,4096]{0,1:T(8,128)(2,1)} copy(bf16[512,4096]{1,0:T(8,128)(2,1)} %param.8) | data formatting | bytes 8388608 | tf_op args[0]
  23.9 6.5 %copy.19 = bf16[512,8,512]{2,0,1:T(8,128)(2,1)} copy(bf16[512,8,512]{0,2,1:T(8,128)(2,1)} %bitcast.73) | data formatting | bytes 8388608 | tf_op jit(solution)/shard_map/reshape | solution.py:16
  30.4 6.5 %copy.16 = bf16[512,4096]{0,1:T(8,128)(2,1)} copy(bf16[512,4096]{1,0:T(8,128)(2,1)} %param.9) | data formatting | bytes 8388608 | tf_op args[1]
  36.9 6.5 %copy.17 = bf16[512,8,512]{2,0,1:T(8,128)(2,1)} copy(bf16[512,8,512]{0,2,1:T(8,128)(2,1)} %bitcast.74) | data formatting | bytes 8388608 | tf_op jit(solution)/shard_map/reshape | solution.py:16
  46.0 0.0 copy-start.4
  46.0 5.1 %gather_fusion.2 = bf16[8,512,512]{2,1,0:T(8,128)(2,1)} fusion(bf16[512,8,512]{2,0,1:T(8,128)(2,1)} %copy.19, s32[1024]{0:T(1024)S(1)} %get-tuple-element.21), kind=kCustom, calls=%fused_computation.1.clone | custom fusion | bytes 8388640 | tf_op jit(solution)/shard_map/jit(_take)/gather | solution.py:17
  51.1 5.0 %gather_fusion.1 = bf16[8,512,512]{2,1,0:T(8,128)(2,1)} fusion(bf16[512,8,512]{2,0,1:T(8,128)(2,1)} %copy.17, s32[1024]{0:T(1024)S(1)} %get-tuple-element.22), kind=kCustom, calls=%fused_computation.clone | custom fusion | bytes 8388640 | tf_op jit(solution)/shard_map/jit(_take)/gather | solution.py:17
  56.2 218.0 %all-reduce.1 = bf16[2,512,512]{2,1,0:T(8,128)(2,1)S(1)} all-reduce(f32[2,512,512]{2,1,0:T(8,128)S(1)} %bitcast_convert_fusion), channel_id=1, replica_groups=mesh['dp'=8,'mp'=32] {'dp'}, use_global_device_ids=true, to_apply=%region_1.2 | all-reduce | flops 524288 | bytes 3145728 | tf_op jit(solution)/shard_map/psum | solution.py:37
  274.2 0.0 all-gather.2.cloned.1.call-done
  274.2 10.5 %gather_fusion = bf16[16,512,512]{2,1,0:T(8,128)(2,1)} fusion(bf16[32,512,512]{2,1,0:T(8,128)(2,1)} %all-gather.2.cloned.1.call-done, s32[1024]{0:T(1024)S(1)} %pad_clamp_fusion.2), kind=kCustom, calls=%fused_computation.2 | custom fusion | bytes 16777280 | tf_op jit(solution)/shard_map/jit(_take)/gather | solution.py:39
  284.7 7.6 %broadcast_select_fusion = bf16[16,512,512]{2,1,0:T(8,128)(2,1)} fusion(bf16[16,512,512]{2,1,0:T(8,128)(2,1)} %gather_fusion, pred[16]{0:T(512)(128)(4,1)S(1)} %compare_and_fusion.2), kind=kLoop, calls=%fused_computation.5 | loop fusion | flops 4194304 | bytes 16777232 | tf_op jit(solution)/shard_map/jit(_take)/select_n | solution.py:39
  292.4 0.0 copy-done.1
  292.4 4.7 %multiply_reduce_fusion = f32[8,512]{1,0:T(8,128)S(1)} fusion(bf16[16,512,512]{2,1,0:T(8,128)(2,1)} %broadcast_select_fusion, bf16[8,512,512]{2,1,0:T(8,128)(2,1)S(1)} %copy-done.1, pred[8]{0:T(512)(128)(4,1)S(1)} %get-tuple-element.15), kind=kOutput, calls=%fused_computation.3 | convolution fusion | flops 2153771008 | bytes 8405000 | tf_op jit(solution)/shard_map/tbi,bij->tbj/dot_general | solution.py:18
  297.1 1.1 copy-done.2
  298.2 2.4 multiply_reduce_fusion.1
  300.6 91.7 %psum.15 = f32[2,8,512]{2,1,0:T(8,128)S(1)} all-reduce(f32[2,8,512]{2,1,0:T(8,128)S(1)} %pad_maximum_fusion.1), channel_id=1, replica_groups=mesh['dp'=8,'mp'=32] {'dp','mp'}, use_global_device_ids=true, to_apply=%region_5.7 | all-reduce | flops 8192 | bytes 65536 | tf_op jit(solution)/shard_map/psum | solution.py:50
  392.3 0.6 fusion.52
  392.9 7.5 %broadcast_select_fusion.1 = bf16[2,8,512,512]{3,2,1,0:T(8,128)(2,1)} fusion(bf16[2,8,512,512]{3,2,1,0:T(8,128)(2,1)} %bitcast.72, pred[2,8]{1,0:T(4,128)(4,1)S(1)} %broadcast_in_dim.31), kind=kLoop, calls=%fused_computation.6 | loop fusion | flops 4194304 | bytes 16777232 | tf_op jit(solution)/shard_map/jit(_take)/select_n | solution.py:39
  400.4 1.9 fusion.10
  402.3 1.9 fusion.12
  404.3 1.9 fusion.11
  406.2 1.9 fusion.13
  408.1 1.1 pad_maximum_fusion
  (13 shorter events, 0.1 us)
Async XLA Ops:
  7.2 267.0 %all-gather.2.cloned.1.call-start = ((), (), s32[]{:S(2)}) async-start(), calls=%async_computation | async-start | bytes 17301504 | tf_op jit(solution)/shard_map/all_gather | solution.py:38
  30.4 15.6 %copy-start.3 = (s32[2,8]{1,0:T(2,128)S(1)}, s32[2,8]{1,0:T(2,128)}, u32[]{:S(2)}) copy-start(s32[2,8]{1,0:T(2,128)} %param.12) | copy-start | bytes 196
  46.0 10.1 %copy-start.4 = (s32[16]{0:T(128)S(1)}, s32[16]{0:T(128)}, u32[]{:S(2)}) copy-start(s32[16]{0:T(128)} %param.13) | copy-start | bytes 196
  284.7 7.6 %copy-start.1 = (bf16[8,512,512]{2,1,0:T(8,128)(2,1)S(1)}, bf16[8,512,512]{2,1,0:T(8,128)(2,1)}, u32[]{:S(2)}) copy-start(bf16[8,512,512]{2,1,0:T(8,128)(2,1)} %gather_fusion.2) | copy-start | bytes 12582916
  292.4 4.7 %copy-start = (bf16[16,512,512]{2,1,0:T(8,128)(2,1)S(1)}, bf16[16,512,512]{2,1,0:T(8,128)(2,1)}, u32[]{:S(2)}) copy-start(bf16[16,512,512]{2,1,0:T(8,128)(2,1)} %broadcast_select_fusion) | copy-start | bytes 25165828
  292.4 5.8 %copy-start.2 = (bf16[8,512,512]{2,1,0:T(8,128)(2,1)S(1)}, bf16[8,512,512]{2,1,0:T(8,128)(2,1)}, u32[]{:S(2)}) copy-start(bf16[8,512,512]{2,1,0:T(8,128)(2,1)} %gather_fusion.1) | copy-start | bytes 12582916
Sparse Core Ops, SparseCore 0:
  9.9 245.4 all-gather.1
where the time goes:
time: 417 us; the launch traced here: 416 us
  blocking collectives  310 us (74%)
  local copies, waits for them, and re-layouts  49.8 us (12%)
  between operations  22 us (5%)
  other arithmetic  19.1 us (5%)
  matrix products  14.8 us (4%)
    psum x1, blocking collectives, local(): lax.psum(grad_parts[0].astype(jnp.float32), 'dp').astype(jnp.bfloat16)  218 us
    psum x1, blocking collectives, local(): eigenvalues = lax.psum(moments, ('dp', 'mp')) / token_count  91.7 us
    select_n x3, other arithmetic, local(): picked = jnp.take(gathered, owners, axis=0)  15.1 us
    unnamed x12, local copies, waits for them, and re-layouts  14.1 us
    reshape x2, local copies, waits for them, and re-layouts, side_moments(): blocks = values.reshape(values.shape[0], placing.shape[0], -1)  12.9 us
    gather x1, local copies, waits for them, and re-layouts, local(): picked = jnp.take(gathered, owners, axis=0)  10.5 us
    gather x2, local copies, waits for them, and re-layouts, side_moments(): selected = jnp.take(blocks, placing, axis=1)  10.1 us
  transfers between devices with their start and end apart: 1, of which 0 were waited for; matrix products, arithmetic and copies ran while one was open for 10% of the time, Pallas kernels for 0%

commit v1 on v0

v1 whole, which is shorter than its diff:
```python
import jax
import jax.numpy as jnp
from jax import lax
from jax.experimental import pallas as pl
from jax.experimental.pallas import tpu as pltpu
from jax.sharding import PartitionSpec as P

DAMPING = 0.5
NB = 8
BS = 512
RING = 4
PIECE = BS // RING
ROWS = PIECE // RING
TILE = 512
MESH = pl.DeviceIdType.MESH
N_SEMS = 128


def kernel(token_count, pattern, owners, tokens, outgrads, grads, slot, precond, eigen_out,
           values, bases, picked, own_grads, grad_in, part_out, part_in, summed, rotated,
           eig, eig_x, eig_y, eig_z, both, send_sems, recv_sems, local_sems):
    dp, mp = lax.axis_index("dp"), lax.axis_index("mp")
    y, z_hi = dp // 2, dp % 2
    core, x, z_lo = mp % 2, (mp // 2) % RING, mp // (2 * RING)
    z = z_hi * RING + z_lo
    side_row = z_lo * (1 - core) + x * core
    side_col = x * (1 - core) + z_lo * core

    def device(dx=0, dy=0, dz=0, dc=0):
        tx, ty, tz = (x + dx + 8) % 4, (y + dy + 8) % 4, (z + dz + 16) % 8
        tc = (core + dc) % 2
        return (ty * 2 + tz // 4, ((tz % 4) * 4 + tx) * 2 + tc)

    def along_row(d):
        return device(dx=d * core, dz=d * (1 - core))

    def along_col(d):
        return device(dx=d * (1 - core), dz=d * core)

    sibling = device(dc=1)
    count = [0]
    pending = []

    def remote(src, dst, target, again=False):
        if not again:
            count[0] += 1
        n = count[0]
        return pltpu.make_async_remote_copy(
            src_ref=src, dst_ref=dst, send_sem=send_sems.at[n], recv_sem=recv_sems.at[n],
            device_id=target, device_id_type=MESH)

    def go(copy):
        copy.start()
        pending.append(copy)
        return copy

    def flush():
        for copy in pending:
            copy.wait_send()
        pending.clear()

    far = 2 - 4 * core
    plane = [(dx, dz) for dz in (1, -1, 0, None) for dx in (1, 3, 0, 2) if dx or dz != 0]
    offsets = [dict(dx=dx, dz=far if dz is None else dz) for dx, dz in plane]
    offsets += [dict(dz=-far), dict(dz=3), dict(dz=-3), dict(dz=4)]
    offsets += [dict(dy=1), dict(dy=3), dict(dy=2)]
    offsets += [dict(dc=1)]

    locals_ = []

    def local(n, src, dst):
        copy = pltpu.make_async_copy(src, dst, local_sems.at[n])
        copy.start()
        return copy

    tokens_here = tokens.shape[0]
    mine = values.at[pl.ds(0, tokens_here)]
    theirs = values.at[pl.ds(tokens_here, tokens_here)]
    chip = z_lo * RING + x

    def piece(row, col):
        return slot.at[pl.ds(pl.multiple_of(row * PIECE + y * ROWS, ROWS), ROWS),
                       pl.ds(pl.multiple_of(col * PIECE, PIECE), PIECE)]

    own_a = local(0, piece(side_row, side_col), picked.at[0, chip])
    own_b = local(1, piece(side_col, side_row), picked.at[2, chip])
    own_g = local(2, grads.at[0, :, pl.ds(pl.multiple_of(y * PIECE, PIECE), PIECE)], own_grads)

    @pl.when(core == 0)
    def _():
        pltpu.make_async_copy(outgrads, mine, local_sems.at[3]).start()

    @pl.when(core == 1)
    def _():
        pltpu.make_async_copy(tokens, mine, local_sems.at[3]).start()

    barrier = pltpu.get_barrier_semaphore()
    for off in offsets:
        back = {k: -v for k, v in off.items()}
        pl.semaphore_signal(barrier, inc=1, device_id=device(**back), device_id_type=MESH)
    pl.semaphore_wait(barrier, len(offsets))

    scatter = []
    for dx, dz in plane:
        dz = far if dz is None else dz
        tx, tz = (x + dx) % 4, (z + dz + 16) % 4
        row = tz * (1 - core) + tx * core
        col = tx * (1 - core) + tz * core
        target = device(dx=dx, dz=dz)
        scatter.append(go(remote(piece(row, col), picked.at[0, chip], target)))
        scatter.append(go(remote(piece(col, row), picked.at[2, chip], target)))

    cross_values = remote(tokens, theirs, sibling)
    cross_outgrads = remote(outgrads, theirs, sibling, again=True)

    @pl.when(core == 0)
    def _():
        cross_values.start()

    @pl.when(core == 1)
    def _():
        cross_outgrads.start()

    pending.append(cross_values)

    def send_quarters(block):
        sent = []
        for j, dy in enumerate((1, 3, 2)):
            ty = (y + dy) % 4
            src = grads.at[0, block, pl.ds(pl.multiple_of(ty * PIECE, PIECE), PIECE)]
            sent.append(go(remote(src, grad_in.at[j, block], device(dy=dy))))
        return sent

    quarters = [send_quarters(0)]

    own_a.wait()
    own_b.wait()
    for copy in scatter:
        copy.wait_recv()
    to_sibling = go(remote(picked.at[2], picked.at[1], sibling))
    wanted = []
    for p in range(NB):
        owner = jnp.int32(0)
        for b in range(NB):
            owner += jnp.where(pattern[core, b] == p, owners[core * NB + b], 0)
        wanted.append(jnp.where(owner % 2 == core, 0, 16) + owner // 2)
    to_sibling.wait_recv()
    first_row = pl.multiple_of(side_row * PIECE + y * ROWS, ROWS)
    for p in range(NB):
        index = wanted[p]
        bases[p, side_col, pl.ds(first_row, ROWS), :] = picked[index // 16, index % 16]

    fine = bases.at[pl.ds(0, NB), side_col, pl.ds(first_row, ROWS)]
    fines = [go(remote(fine, fine, device(dy=dy))) for dy in (1, 3, 2)]
    quarters.append(send_quarters(1))
    for copy in fines:
        copy.wait_recv()

    def chunk(row, half=None):
        rows = pl.ds(pl.multiple_of(((side_row + row + 4) % 4) * PIECE, PIECE), PIECE)
        some = pl.ds(0, NB) if half is None else pl.ds(half * (NB // 2), NB // 2)
        return some, rows

    def at(row, col, half=None):
        some, rows = chunk(row, half)
        return bases.at[some, (side_col + col + 4) % 4, rows]

    def send(ref, target):
        return go(remote(ref, ref, target))

    rows_up = send(at(0, 0), along_row(1))
    rows_down = send(at(0, 0), along_row(-1))
    arriving = {}
    for row in (0,):
        arriving[row] = (send(at(row, 0), along_col(1)), send(at(row, 0), along_col(-1)))
    rows_up.wait_recv()
    rows_up_far = send(at(-1, 0, 0), along_row(1))
    rows_down.wait_recv()
    rows_down_far = send(at(1, 0, 1), along_row(-1))
    for row in (-1, 1):
        arriving[row] = (send(at(row, 0), along_col(1)), send(at(row, 0), along_col(-1)))

    z_parts = []
    for block in range(2):
        if block == 0:
            own_g.wait()
        for copy in quarters[block]:
            copy.wait_recv()
        total = own_grads[block].astype(jnp.float32)
        for j in range(3):
            total += grad_in[j, block].astype(jnp.float32)
        part_out[block] = total.astype(jnp.bfloat16)
        z_parts.append(go(remote(part_out.at[block], part_in.at[block], device(dz=4))))

    far_halves = {}

    def pass_on(row):
        up, down = arriving[row]
        up.wait_recv()
        first = send(at(row, -1, 0), along_col(1))
        down.wait_recv()
        second = send(at(row, 1, 1), along_col(-1))
        far_halves[row] = (first, second)

    pass_on(0)
    rows_up_far.wait_recv()
    rows_down_far.wait_recv()
    arriving[2] = (send(at(2, 0), along_col(1)), send(at(2, 0), along_col(-1)))

    own_values = pltpu.make_async_copy(tokens, mine, local_sems.at[3])
    own_values.wait()
    cross_values.wait_recv()

    def project(col):
        place = (side_col + col + 4) % 4
        columns = pl.ds(pl.multiple_of(place * PIECE, PIECE), PIECE)

        def one(p, sums):
            weights = bases[p, place]

            def tile(t, total):
                block = values[pl.ds(pl.multiple_of(t * TILE, TILE), TILE),
                               pl.ds(pl.multiple_of(p * BS, BS), BS)]
                out = jnp.dot(block, weights, preferred_element_type=jnp.float32)
                return total + jnp.sum((out * out).reshape(TILE // 8, 8, PIECE), axis=0)

            total = lax.fori_loop(0, 2 * tokens_here // TILE, tile, jnp.zeros((8, PIECE), jnp.float32))
            here = lax.broadcasted_iota(jnp.int32, (NB, PIECE), 0) == p
            return jnp.where(here, jnp.sum(total, axis=0, keepdims=True), sums)

        eig[:, columns] = lax.fori_loop(0, NB, one, jnp.zeros((NB, PIECE), jnp.float32))

    project(0)
    for row in (-1, 1, 2):
        pass_on(row)
    project(-1)
    project(1)

    own_rows = pl.ds(pl.multiple_of(y * PIECE, PIECE), PIECE)
    whole = []
    for block in range(2):
        z_parts[block].wait_recv()
        total = part_out[block].astype(jnp.float32) + part_in[block].astype(jnp.float32)
        summed[block, own_rows] = total.astype(jnp.bfloat16)
        ref = summed.at[block, own_rows]
        whole += [go(remote(ref, ref, device(dy=dy))) for dy in (1, 3, 2)]

    for row in (0, -1, 1, 2):
        for copy in far_halves[row]:
            copy.wait_recv()
    project(2)

    eig_x[x] = eig[...]
    over_x = [go(remote(eig, eig_x.at[x], device(dx=dx))) for dx in (1, 3, 2)]

    out_place = z_lo * 2 + x // 2
    in_place = (x % 2) * 4
    one_basis = remote(bases.at[out_place], bases.at[NB], sibling)
    two_bases = remote(bases.at[pl.ds(in_place, 2)], bases.at[pl.ds(NB, 2)], sibling)

    @pl.when(core == 0)
    def _():
        one_basis.start()

    @pl.when(core == 1)
    def _():
        two_bases.start()

    for copy in over_x:
        copy.wait_recv()
    eig_y[y] = (eig_x[0] + eig_x[1]) + (eig_x[2] + eig_x[3])
    over_y = [go(remote(eig_y.at[y], eig_y.at[y], device(dy=dy))) for dy in (1, 3, 2)]

    @pl.when(core == 0)
    def _():
        two_bases.wait_recv()
        one_basis.wait_send()

    @pl.when(core == 1)
    def _():
        one_basis.wait_recv()
        two_bases.wait_send()

    for copy in over_y:
        copy.wait_recv()
    eig_z[z] = (eig_y[0] + eig_y[1]) + (eig_y[2] + eig_y[3])
    over_z = [go(remote(eig_z.at[z], eig_z.at[z], device(dz=dz))) for dz in (1, -1, 2, -2, 3, -3, 4)]

    out_basis = out_place * (1 - core) + NB * core

    def in_basis(j):
        return (NB + j) * (1 - core) + (in_place + 2 + j) * core

    def basis(place):
        return jnp.concatenate([bases[place, col] for col in range(RING)], axis=1)

    for copy in whole:
        copy.wait_recv()

    def rotate(j, _):
        halfway = lax.dot_general(basis(out_basis), summed[j], (((0,), (0,)), ((), ())),
                                  preferred_element_type=jnp.float32).astype(jnp.bfloat16)
        rotated[j] = jnp.dot(halfway, basis(in_basis(j)), preferred_element_type=jnp.float32)
        return 0

    lax.fori_loop(0, 2, rotate, 0)
    flush_later = list(pending)
    pending.clear()
    for copy in over_z:
        copy.wait_recv()
    total = (eig_z[0] + eig_z[1]) + (eig_z[2] + eig_z[3])
    total += (eig_z[4] + eig_z[5]) + (eig_z[6] + eig_z[7])
    both[core] = total / token_count
    across = go(remote(both.at[core], both.at[core], sibling))
    across.wait_recv()

    for s in range(2):
        for b in range(NB):
            eigen_out[s * NB + b: s * NB + b + 1, :] = both[s, pl.ds(pattern[s, b], 1), :]

    out_scale = both[0, pl.ds(out_place, 1), :].reshape(BS, 1)

    def finish(j, _):
        in_scale = both[1, pl.ds(in_place + 2 * core + j, 1), :]
        scaled = (rotated[j] / (out_scale * in_scale + DAMPING)).astype(jnp.bfloat16)
        returned = jnp.dot(basis(out_basis), scaled, preferred_element_type=jnp.float32).astype(jnp.bfloat16)
        precond[j] = lax.dot_general(returned, basis(in_basis(j)), (((1,), (1,)), ((), ())),
                                     preferred_element_type=jnp.float32).astype(jnp.bfloat16)
        return 0

    lax.fori_loop(0, 2, finish, 0)
    flush()
    for copy in flush_later:
        copy.wait_send()


def local(token_total, tokens, outgrads, grad_parts, basis_slots, pattern, owners):
    here = tokens.shape[0]
    bf16, f32 = jnp.bfloat16, jnp.float32
    anywhere = pl.BlockSpec(memory_space=pl.ANY)
    scalars = pl.BlockSpec(memory_space=pltpu.SMEM)
    vmem = pl.BlockSpec(memory_space=pltpu.VMEM)

    def body(*refs):
        kernel(float(token_total), *refs)

    return pl.pallas_call(
        body,
        out_shape=(jax.ShapeDtypeStruct((2, BS, BS), bf16), jax.ShapeDtypeStruct((2 * NB, BS), f32)),
        in_specs=[scalars, scalars, anywhere, anywhere, anywhere, anywhere],
        out_specs=(vmem, vmem),
        scratch_shapes=[
            pltpu.VMEM((2 * here, NB * BS), bf16),
            pltpu.VMEM((NB + 2, RING, BS, PIECE), bf16),
            pltpu.VMEM((3, 16, ROWS, PIECE), bf16),
            pltpu.VMEM((2, PIECE, BS), bf16),
            pltpu.VMEM((3, 2, PIECE, BS), bf16),
            pltpu.VMEM((2, PIECE, BS), bf16),
            pltpu.VMEM((2, PIECE, BS), bf16),
            pltpu.VMEM((2, BS, BS), bf16),
            pltpu.VMEM((2, BS, BS), f32),
            pltpu.VMEM((NB, BS), f32),
            pltpu.VMEM((4, NB, BS), f32),
            pltpu.VMEM((4, NB, BS), f32),
            pltpu.VMEM((8, NB, BS), f32),
            pltpu.VMEM((2, NB, BS), f32),
            pltpu.SemaphoreType.DMA((N_SEMS,)),
            pltpu.SemaphoreType.DMA((N_SEMS,)),
            pltpu.SemaphoreType.DMA((4,)),
        ],
        compiler_params=pltpu.CompilerParams(
            collective_id=0, has_side_effects=True, vmem_limit_bytes=48 * 2 ** 20),
    )(pattern, owners, tokens, outgrads, grad_parts, basis_slots.reshape(BS, BS))


def solution(mesh):
    placed = (
        P(("dp", "mp"), None),
        P(("dp", "mp"), None),
        P("dp", "mp", None, None),
        P("mp", None, None),
        P(),
        P(),
    )

    def whole(tokens, *rest):
        total = tokens.shape[0]
        return jax.shard_map(
            lambda *args: local(total, *args), mesh=mesh, in_specs=placed,
            out_specs=(P("mp", None, None), P()), check_vma=False)(tokens, *rest)

    return whole
```

time: 417 us -> 91.4 us (0.22)
  blocking collectives: 310 us -> 0 us
  Pallas kernels: 0 us -> 85.4 us
  local copies, waits for them, and re-layouts: 49.8 us -> 5.18 us
  between operations: 22 us -> 0.65 us
  other arithmetic: 19.1 us -> 0 us
  matrix products: 14.8 us -> 0 us
    psum x2 -> x0, blocking collectives: 310 us -> none  [the longest x1 218 us: local(): lax.psum(grad_parts[0].astype(jnp.float32), 'dp').astype(jnp.bfloat16)]
    pallas_call x0 -> x1, Pallas kernels: none -> 85.4 us  [local(): pl.pallas_call(body, out_shape=(jax.ShapeDtypeStruct((2, BS, BS), bf16),...]
    gather x3 -> x0, local copies, waits for them, and re-layouts: 20.6 us -> none  [the longest x1 10.5 us: local(): picked = jnp.take(gathered, owners, axis=0)]
    select_n x3 -> x0, other arithmetic: 15.1 us -> none  [local(): picked = jnp.take(gathered, owners, axis=0)]
    dot_general x6 -> x0, matrix products: 14.8 us -> none  [the longest x2 7.12 us: side_moments(): jnp.einsum('tbi,bij->tbj', selected, side_bases, preferred_element_type=j...]
    reshape x2 -> x0, local copies, waits for them, and re-layouts: 12.9 us -> none  [side_moments(): blocks = values.reshape(values.shape[0], placing.shape[0], -1)]
    unnamed x12 -> x10, local copies, waits for them, and re-layouts: 14.1 us -> 5.18 us
  transfers between devices with their start and end apart: 1 -> 0, of which waited for: 0 -> 0; matrix products, arithmetic and copies ran while one was open for 10% -> 0% of each run, Pallas kernels for 0% -> 0%
where the time goes in v1:
time: 91.4 us; the launch traced here: 91.2 us
  Pallas kernels  85.4 us (93%)
  local copies, waits for them, and re-layouts  5.18 us (6%)
    pallas_call x1, Pallas kernels, local(): pl.pallas_call(body, out_shape=(jax.ShapeDtypeStruct((2, BS, BS), bf16),...  85.4 us
    unnamed x10, local copies, waits for them, and re-layouts  5.18 us

profile of v1, /device:TPU:1, one launch (start us, length us, event | category | flops | bytes accessed | tf_op | source)
XLA Modules:
  0.0 91.2 jit_solution(1371165495593498840)
XLA Ops:
  0.6 0.0 copy-start
  0.6 1.2 %copy-done = bf16[1,2,512,512]{3,2,1,0:T(8,128)(2,1)S(1)} copy-done((bf16[1,2,512,512]{3,2,1,0:T(8,128)(2,1)S(1)}, bf16[1,2,512,512]{3,2,1,0:T(8,128)(2,1)}, u32[]{:S(2)}) %copy-start) | copy-done | bytes 1048600
  1.9 0.0 copy-start.1
  1.9 1.0 %copy-done.1 = bf16[1,512,512]{2,1,0:T(8,128)(2,1)S(1)} copy-done((bf16[1,512,512]{2,1,0:T(8,128)(2,1)S(1)}, bf16[1,512,512]{2,1,0:T(8,128)(2,1)}, u32[]{:S(2)}) %copy-start.1) | copy-done | bytes 524312
  2.9 0.0 copy-start.2
  2.9 0.7 copy-done.2
  3.6 0.0 copy-start.3
  3.6 0.7 copy-done.3
  4.2 85.4 %shard_map.77 = (bf16[2,512,512]{2,1,0:T(8,128)(2,1)S(1)}, f32[16,512]{1,0:T(8,128)S(1)}) custom-call(s32[2,8]{1,0:T(2,128)S(1)} %copy-done.2, s32[16]{0:T(128)S(1)} %copy-done.3, bf16[512,4096]{1,0:T(8,128)(2,1)} %refs_2_.1, bf16[512,4096]{1,0:T(8,128)(2,1)} %refs_3_.1, bf16[1,2,512,512]{3,2,1,0:T(8,128)(2,1)S(1)} %copy-done, bf16[512,512]{1,0:T(8,128)(2,1)S(1)} %bitcast.1), custom_call_target="tpu_custom_call" | custom-call | tf_op jit(solution)/shard_map/pallas_call | solution.py:347
  89.6 1.0 %copy.10 = bf16[2,512,512]{2,1,0:T(8,128)(2,1)} copy(bf16[2,512,512]{2,1,0:T(8,128)(2,1)S(1)} %get-tuple-element.4) | data formatting | bytes 2097152
  90.6 0.6 copy.11
Async XLA Ops:
  0.6 1.2 %copy-start = (bf16[1,2,512,512]{3,2,1,0:T(8,128)(2,1)S(1)}, bf16[1,2,512,512]{3,2,1,0:T(8,128)(2,1)}, u32[]{:S(2)}) copy-start(bf16[1,2,512,512]{3,2,1,0:T(8,128)(2,1)} %refs_4_.1) | copy-start | bytes 3145732
  1.9 1.0 %copy-start.1 = (bf16[1,512,512]{2,1,0:T(8,128)(2,1)S(1)}, bf16[1,512,512]{2,1,0:T(8,128)(2,1)}, u32[]{:S(2)}) copy-start(bf16[1,512,512]{2,1,0:T(8,128)(2,1)} %param.9) | copy-start | bytes 1572868
  2.9 0.7 copy-start.2
  3.6 0.7 copy-start.3

commit v2 on v1

v2 whole, which is shorter than its diff:
```python
import jax
import jax.numpy as jnp
from jax import lax
from jax.experimental import pallas as pl
from jax.experimental.pallas import tpu as pltpu
from jax.sharding import PartitionSpec as P

DAMPING = 0.5
NB = 8
BS = 512
RING = 4
PIECE = BS // RING
ROWS = PIECE // RING
MESH = pl.DeviceIdType.MESH
N_SEMS = 128


class Far:
    def __init__(self, sign):
        self.sign = sign

    def __neg__(self):
        return Far(-self.sign)


def kernel(token_count, pattern_in, owners_in, tokens, outgrads, grads, slot, precond, eigen_out,
           pattern, owners, values, bases, picked, own_grads, grad_in, part_out, part_in, summed, rotated,
           eig, eig_x, eig_y, eig_z, both, send_sems, recv_sems, local_sems):
    dp, mp = lax.axis_index("dp"), lax.axis_index("mp")
    y, z_hi = lax.div(dp, 2), lax.rem(dp, 2)
    core, chip = lax.rem(mp, 2), lax.div(mp, 2)
    x, z_lo = lax.rem(chip, RING), lax.div(chip, RING)
    z = z_hi * RING + z_lo
    known = {}

    def wrapped(name, value, delta, size):
        if (name, delta) not in known:
            known[name, delta] = lax.rem(value + (delta + size), size) if delta else value
        return known[name, delta]

    def mp_part(dx, dz):
        if ("mp", dx, dz) not in known:
            known["mp", dx, dz] = wrapped("z_lo", z_lo, dz % 4, 4) * 8 + wrapped("x", x, dx % 4, 4) * 2
        return known["mp", dx, dz]

    def dp_part(dy, dz):
        if ("dp", dy, dz) not in known:
            known["dp", dy, dz] = wrapped("y", y, dy % 4, 4) * 2 + lax.div(wrapped("z", z, dz % 8, 8), 4)
        return known["dp", dy, dz]
    side_row = z_lo * (1 - core) + x * core
    side_col = x * (1 - core) + z_lo * core

    def device(dx=0, dy=0, dz=0, dc=0):
        if isinstance(dz, Far):
            first, second = device(dx, dy, 2 * dz.sign, dc), device(dx, dy, -2 * dz.sign, dc)
            return tuple(a + (b - a) * core for a, b in zip(first, second))
        return (dp_part(dy, dz), mp_part(dx, dz) + (core if dc == 0 else 1 - core))

    def along(d):
        if ("along", d) not in known:
            over_x, over_z = device(dx=d), device(dz=d)
            known["along", d] = (
                tuple(b + (a - b) * core for a, b in zip(over_x, over_z)),
                tuple(a + (b - a) * core for a, b in zip(over_x, over_z)))
        return known["along", d]

    def along_row(d):
        return along(d)[0]

    def along_col(d):
        return along(d)[1]

    sibling = device(dc=1)
    count = [0]
    pending = []

    def remote(src, dst, target, again=False):
        if not again:
            count[0] += 1
        n = count[0]
        return pltpu.make_async_remote_copy(
            src_ref=src, dst_ref=dst, send_sem=send_sems.at[n], recv_sem=recv_sems.at[n],
            device_id=target, device_id_type=MESH)

    def go(copy):
        copy.start()
        pending.append(copy)
        return copy

    def flush():
        for copy in pending:
            copy.wait_send()
        pending.clear()

    far = Far(1)
    plane = [(dx, dz) for dz in (1, -1, 0, far) for dx in (1, 3, 0, 2) if dx or dz != 0]
    offsets = [dict(dx=dx, dz=dz) for dx, dz in plane]
    offsets += [dict(dz=-far), dict(dz=3), dict(dz=-3), dict(dz=4)]
    offsets += [dict(dy=1), dict(dy=3), dict(dy=2)]
    offsets += [dict(dc=1)]

    def local(n, src, dst):
        copy = pltpu.make_async_copy(src, dst, local_sems.at[n])
        copy.start()
        return copy

    tokens_here = tokens.shape[0]
    mine = values.at[pl.ds(0, tokens_here)]
    theirs = values.at[pl.ds(tokens_here, tokens_here)]
    def piece(row, col):
        return slot.at[pl.ds(pl.multiple_of(row * PIECE + y * ROWS, ROWS), ROWS),
                       pl.ds(pl.multiple_of(col * PIECE, PIECE), PIECE)]

    own_p = local(4, pattern_in, pattern)
    own_o = local(5, owners_in, owners)
    own_a = local(0, piece(side_row, side_col), picked.at[0, chip])
    own_b = local(1, piece(side_col, side_row), picked.at[2, chip])
    own_g = local(2, grads.at[0, :, pl.ds(pl.multiple_of(y * PIECE, PIECE), PIECE)], own_grads)

    @pl.when(core == 0)
    def _():
        pltpu.make_async_copy(outgrads, mine, local_sems.at[3]).start()

    @pl.when(core == 1)
    def _():
        pltpu.make_async_copy(tokens, mine, local_sems.at[3]).start()

    barrier = pltpu.get_barrier_semaphore()
    for off in offsets:
        back = {k: -v for k, v in off.items()}
        pl.semaphore_signal(barrier, inc=1, device_id=device(**back), device_id_type=MESH)
    pl.semaphore_wait(barrier, len(offsets))

    scatter = []
    for dx, dz in plane:
        tx = wrapped("x", x, dx, 4)
        tz = wrapped("z_lo", z_lo, 2 if dz is far else dz % 4, 4)
        row = tz * (1 - core) + tx * core
        col = tx * (1 - core) + tz * core
        target = device(dx=dx, dz=dz)
        scatter.append(go(remote(piece(row, col), picked.at[0, chip], target)))
        scatter.append(go(remote(piece(col, row), picked.at[2, chip], target)))

    def send_quarters(block):
        sent = []
        for j, dy in enumerate((1, 3, 2)):
            ty = wrapped("y", y, dy, 4)
            src = grads.at[0, block, pl.ds(pl.multiple_of(ty * PIECE, PIECE), PIECE)]
            sent.append(go(remote(src, grad_in.at[j, block], device(dy=dy))))
        return sent

    quarters = [send_quarters(0)]

    for copy in (own_p, own_o, own_a, own_b):
        copy.wait()
    for copy in scatter:
        copy.wait_recv()
    to_sibling = go(remote(picked.at[2], picked.at[1], sibling))
    wanted = []
    for p in range(NB):
        owner = jnp.int32(0)
        for b in range(NB):
            owner += jnp.where(pattern[core, b] == p, owners[core * NB + b], 0)
        wanted.append((jnp.where(lax.rem(owner, 2) == core, 0, 1), lax.div(owner, 2)))
    to_sibling.wait_recv()
    for p in range(NB):
        bases[p, side_col, side_row, 0] = picked[wanted[p]]

    def unit(row, col, quarters, half=None):
        some = pl.ds(0, NB) if half is None else pl.ds(half * (NB // 2), NB // 2)
        place = wrapped("col", side_col, col % 4, 4), wrapped("row", side_row, row % 4, 4)
        return bases.at[some, place[0], place[1], pl.ds(*quarters)]

    def send(ref, target):
        return go(remote(ref, ref, target))

    own, rest = (0, 1), (1, 3)
    over_rows, over_cols, far_cols = {}, {}, {}

    def both_ways(row, part):
        over_cols[row, part] = (send(unit(row, 0, part), along_col(1)), send(unit(row, 0, part), along_col(-1)))

    def have_own(row):
        over_rows[row] = [
            go(remote(unit(row, 0, own), unit(row, 0, (4 - dy, 1)), device(dy=dy))) for dy in (1, 3, 2)]
        both_ways(row, own)

    def have_rest(row):
        for copy in over_rows[row]:
            copy.wait_recv()
        both_ways(row, rest)

    def pass_on(row, part):
        up, down = over_cols[row, part]
        up.wait_recv()
        first = send(unit(row, -1, part, 0), along_col(1))
        down.wait_recv()
        second = send(unit(row, 1, part, 1), along_col(-1))
        far_cols[row, part] = (first, second)

    rows_up = send(unit(0, 0, own), along_row(1))
    rows_down = send(unit(0, 0, own), along_row(-1))
    have_own(0)
    cross_values = remote(tokens, theirs, sibling)
    cross_outgrads = remote(outgrads, theirs, sibling, again=True)

    @pl.when(core == 0)
    def _():
        cross_values.start()

    @pl.when(core == 1)
    def _():
        cross_outgrads.start()

    pending.append(cross_values)

    z_parts = []

    def partial_sum(block):
        if block == 0:
            own_g.wait()
        for copy in quarters[block]:
            copy.wait_recv()
        total = own_grads[block].astype(jnp.float32)
        for j in range(3):
            total += grad_in[j, block].astype(jnp.float32)
        part_out[block] = total.astype(jnp.bfloat16)
        z_parts.append(go(remote(part_out.at[block], part_in.at[block], device(dz=4))))

    rows_up.wait_recv()
    rows_up_far = send(unit(-1, 0, own, 0), along_row(1))
    rows_down.wait_recv()
    rows_down_far = send(unit(1, 0, own, 1), along_row(-1))
    have_own(-1)
    have_own(1)
    pass_on(0, own)
    have_rest(0)
    rows_up_far.wait_recv()
    rows_down_far.wait_recv()
    have_own(2)
    quarters.append(send_quarters(1))
    pass_on(-1, own)
    pass_on(1, own)
    partial_sum(0)
    have_rest(-1)
    pass_on(0, rest)
    have_rest(1)
    pass_on(2, own)
    have_rest(2)

    own_values = pltpu.make_async_copy(tokens, mine, local_sems.at[3])
    own_values.wait()
    cross_values.wait_recv()

    turned = [lax.rem(k + 4 - y, 4) for k in range(4)]

    def columns_of(p, place):
        return jnp.concatenate([bases[p, place, row, turn] for row in range(RING) for turn in turned], axis=0)

    def project(*cols):
        places = [wrapped("col", side_col, col % 4, 4) for col in cols]
        width = PIECE * len(cols)

        def one(p, sums):
            weights = jnp.concatenate([columns_of(p, place) for place in places], axis=1)
            block = values[:, pl.ds(pl.multiple_of(p * BS, BS), BS)]
            out = jnp.dot(block, weights, preferred_element_type=jnp.float32)
            total = jnp.sum((out * out).reshape(2 * tokens_here // 8, 8, width), axis=0)
            here = lax.broadcasted_iota(jnp.int32, (NB, width), 0) == p
            return jnp.where(here, jnp.sum(total, axis=0, keepdims=True), sums)

        sums = lax.fori_loop(0, NB, one, jnp.zeros((NB, width), jnp.float32), unroll=4)
        for n, place in enumerate(places):
            columns = pl.ds(pl.multiple_of(place * PIECE, PIECE), PIECE)
            eig[:, columns] = sums[:, n * PIECE:(n + 1) * PIECE]

    pass_on(-1, rest)
    project(0)
    pass_on(1, rest)
    pass_on(2, rest)
    project(-1, 1)
    partial_sum(1)

    for copies in far_cols.values():
        for copy in copies:
            copy.wait_recv()
    project(2)

    eig_x[x] = eig[...]
    over_x = [go(remote(eig, eig_x.at[x], device(dx=dx))) for dx in (1, 3, 2)]

    own_rows = pl.ds(pl.multiple_of(y * PIECE, PIECE), PIECE)
    whole = []
    for block in range(2):
        z_parts[block].wait_recv()
        total = part_out[block].astype(jnp.float32) + part_in[block].astype(jnp.float32)
        summed[block, own_rows] = total.astype(jnp.bfloat16)
        ref = summed.at[block, own_rows]
        whole += [go(remote(ref, ref, device(dy=dy))) for dy in (1, 3, 2)]

    out_place = z_lo * 2 + lax.div(x, 2)
    in_place = lax.rem(x, 2) * 4
    one_basis = remote(bases.at[out_place], bases.at[NB], sibling)
    two_bases = remote(bases.at[pl.ds(in_place, 2)], bases.at[pl.ds(NB, 2)], sibling)

    @pl.when(core == 0)
    def _():
        one_basis.start()

    @pl.when(core == 1)
    def _():
        two_bases.start()

    for copy in over_x:
        copy.wait_recv()
    eig_y[y] = (eig_x[0] + eig_x[1]) + (eig_x[2] + eig_x[3])
    over_y = [go(remote(eig_y.at[y], eig_y.at[y], device(dy=dy))) for dy in (1, 3, 2)]

    @pl.when(core == 0)
    def _():
        two_bases.wait_recv()
        one_basis.wait_send()

    @pl.when(core == 1)
    def _():
        one_basis.wait_recv()
        two_bases.wait_send()

    for copy in over_y:
        copy.wait_recv()
    eig_z[z] = (eig_y[0] + eig_y[1]) + (eig_y[2] + eig_y[3])
    over_z = [go(remote(eig_z.at[z], eig_z.at[z], device(dz=dz))) for dz in (1, -1, 2, -2, 3, -3, 4)]

    out_basis = out_place * (1 - core) + NB * core

    def in_basis(j):
        return (NB + j) * (1 - core) + (in_place + 2 + j) * core

    def basis(place):
        return jnp.concatenate([columns_of(place, col) for col in range(RING)], axis=1)

    for copy in whole:
        copy.wait_recv()

    def rotate(j, _):
        halfway = lax.dot_general(basis(out_basis), summed[j], (((0,), (0,)), ((), ())),
                                  preferred_element_type=jnp.float32).astype(jnp.bfloat16)
        rotated[j] = jnp.dot(halfway, basis(in_basis(j)), preferred_element_type=jnp.float32)
        return 0

    lax.fori_loop(0, 2, rotate, 0)
    flush_later = list(pending)
    pending.clear()
    for copy in over_z:
        copy.wait_recv()
    total = (eig_z[0] + eig_z[1]) + (eig_z[2] + eig_z[3])
    total += (eig_z[4] + eig_z[5]) + (eig_z[6] + eig_z[7])
    both[core] = total / token_count
    across = go(remote(both.at[core], both.at[core], sibling))
    across.wait_recv()

    for s in range(2):
        for b in range(NB):
            eigen_out[s * NB + b: s * NB + b + 1, :] = both[s, pl.ds(pattern[s, b], 1), :]

    out_scale = both[0, pl.ds(out_place, 1), :].reshape(BS, 1)

    def finish(j, _):
        in_scale = both[1, pl.ds(in_place + 2 * core + j, 1), :]
        scaled = (rotated[j] / (out_scale * in_scale + DAMPING)).astype(jnp.bfloat16)
        returned = jnp.dot(basis(out_basis), scaled, preferred_element_type=jnp.float32).astype(jnp.bfloat16)
        precond[j] = lax.dot_general(returned, basis(in_basis(j)), (((1,), (1,)), ((), ())),
                                     preferred_element_type=jnp.float32).astype(jnp.bfloat16)
        return 0

    lax.fori_loop(0, 2, finish, 0)
    flush()
    for copy in flush_later:
        copy.wait_send()


def local(token_total, tokens, outgrads, grad_parts, basis_slots, pattern, owners):
    here = tokens.shape[0]
    bf16, f32 = jnp.bfloat16, jnp.float32
    anywhere = pl.BlockSpec(memory_space=pl.ANY)
    vmem = pl.BlockSpec(memory_space=pltpu.VMEM)

    def body(*refs):
        kernel(float(token_total), *refs)

    operands = (pattern, owners, tokens, outgrads, grad_parts, basis_slots.reshape(BS, BS))
    return pl.pallas_call(
        body,
        out_shape=(jax.ShapeDtypeStruct((2, BS, BS), bf16), jax.ShapeDtypeStruct((2 * NB, BS), f32)),
        in_specs=[anywhere] * 6,
        out_specs=(vmem, vmem),
        scratch_shapes=[
            pltpu.SMEM((2, NB), jnp.int32),
            pltpu.SMEM((2 * NB,), jnp.int32),
            pltpu.VMEM((2 * here, NB * BS), bf16),
            pltpu.VMEM((NB + 2, RING, RING, RING, ROWS, PIECE), bf16),
            pltpu.VMEM((3, 16, ROWS, PIECE), bf16),
            pltpu.VMEM((2, PIECE, BS), bf16),
            pltpu.VMEM((3, 2, PIECE, BS), bf16),
            pltpu.VMEM((2, PIECE, BS), bf16),
            pltpu.VMEM((2, PIECE, BS), bf16),
            pltpu.VMEM((2, BS, BS), bf16),
            pltpu.VMEM((2, BS, BS), f32),
            pltpu.VMEM((NB, BS), f32),
            pltpu.VMEM((4, NB, BS), f32),
            pltpu.VMEM((4, NB, BS), f32),
            pltpu.VMEM((8, NB, BS), f32),
            pltpu.VMEM((2, NB, BS), f32),
            pltpu.SemaphoreType.DMA((N_SEMS,)),
            pltpu.SemaphoreType.DMA((N_SEMS,)),
            pltpu.SemaphoreType.DMA((6,)),
        ],
        compiler_params=pltpu.CompilerParams(
            collective_id=0, has_side_effects=True, vmem_limit_bytes=48 * 2 ** 20),
    )(*[pltpu.with_memory_space_constraint(operand, pltpu.HBM) for operand in operands])


def solution(mesh):
    placed = (
        P(("dp", "mp"), None),
        P(("dp", "mp"), None),
        P("dp", "mp", None, None),
        P("mp", None, None),
        P(),
        P(),
    )

    def whole(tokens, *rest):
        total = tokens.shape[0]
        return jax.shard_map(
            lambda *args: local(total, *args), mesh=mesh, in_specs=placed,
            out_specs=(P("mp", None, None), P()), check_vma=False)(tokens, *rest)

    return whole
```

time: 91.4 us -> 74.3 us (0.81)
  Pallas kernels: 85.4 us -> 72 us
  local copies, waits for them, and re-layouts: 5.18 us -> 1.59 us
    pallas_call x1, Pallas kernels: 85.4 us -> 72 us  [local(): pl.pallas_call(body, out_shape=(jax.ShapeDtypeStruct((2, BS, BS), bf16),...]
    unnamed x10 -> x2, local copies, waits for them, and re-layouts: 5.18 us -> 1.59 us
where the time goes in v2:
time: 74.3 us; the launch traced here: 74.2 us
  Pallas kernels  72 us (97%)
  local copies, waits for them, and re-layouts  1.59 us (2%)
    pallas_call x1, Pallas kernels, local(): pl.pallas_call(body, out_shape=(jax.ShapeDtypeStruct((2, BS, BS), bf16),...  72 us
    unnamed x2, local copies, waits for them, and re-layouts  1.59 us

profile of v2, /device:TPU:1, one launch (start us, length us, event | category | flops | bytes accessed | tf_op | source)
XLA Modules:
  0.0 74.2 jit_solution(18409336933369252987)
XLA Ops:
  0.6 72.0 %shard_map.77 = (bf16[2,512,512]{2,1,0:T(8,128)(2,1)S(1)}, f32[16,512]{1,0:T(8,128)S(1)}) custom-call(s32[2,8]{1,0:T(2,128)} %refs_0_.1, s32[16]{0:T(128)} %refs_1_.1, bf16[512,4096]{1,0:T(8,128)(2,1)} %refs_2_.1, bf16[512,4096]{1,0:T(8,128)(2,1)} %refs_3_.1, bf16[1,2,512,512]{3,2,1,0:T(8,128)(2,1)} %refs_4_.1, bf16[512,512]{1,0:T(8,128)(2,1)} %bitcast.1), custom_call_target="tpu_custom_call" | custom-call | tf_op jit(solution)/shard_map/pallas_call | solution.py:392
  72.6 1.0 %copy.10 = bf16[2,512,512]{2,1,0:T(8,128)(2,1)} copy(bf16[2,512,512]{2,1,0:T(8,128)(2,1)S(1)} %get-tuple-element.4) | data formatting | bytes 2097152
  73.6 0.6 copy.11

commit v3 on v2

--- a/solution.py
+++ b/solution.py
@@ -24,7 +24,7 @@
 
 
 def kernel(token_count, pattern_in, owners_in, tokens, outgrads, grads, slot, precond, eigen_out,
-           pattern, owners, values, bases, picked, own_grads, grad_in, part_out, part_in, summed, rotated,
+           pattern, owners, slot_quarter, values, bases, picked, own_grads, grad_in, part_out, part_in, summed, rotated,
            eig, eig_x, eig_y, eig_z, both, send_sems, recv_sems, local_sems):
     dp, mp = lax.axis_index("dp"), lax.axis_index("mp")
     y, z_hi = lax.div(dp, 2), lax.rem(dp, 2)
@@ -93,7 +93,9 @@
         pending.clear()
 
     far = Far(1)
-    plane = [(dx, dz) for dz in (1, -1, 0, far) for dx in (1, 3, 0, 2) if dx or dz != 0]
+    plane = [(dx, dz) for dz in (far, 1, -1, 0) for dx in (2, 1, 3, 0) if dx or dz != 0]
+    hops = {0: 0, 1: 1, -1: 1, 2: 2, 3: 1, far: 2}
+    plane.sort(key=lambda step: -hops[step[0]] - hops[step[1]])
     offsets = [dict(dx=dx, dz=dz) for dx, dz in plane]
     offsets += [dict(dz=-far), dict(dz=3), dict(dz=-3), dict(dz=4)]
     offsets += [dict(dy=1), dict(dy=3), dict(dy=2)]
@@ -107,30 +109,42 @@
     tokens_here = tokens.shape[0]
     mine = values.at[pl.ds(0, tokens_here)]
     theirs = values.at[pl.ds(tokens_here, tokens_here)]
+
     def piece(row, col):
-        return slot.at[pl.ds(pl.multiple_of(row * PIECE + y * ROWS, ROWS), ROWS),
-                       pl.ds(pl.multiple_of(col * PIECE, PIECE), PIECE)]
-
-    own_p = local(4, pattern_in, pattern)
-    own_o = local(5, owners_in, owners)
-    own_a = local(0, piece(side_row, side_col), picked.at[0, chip])
-    own_b = local(1, piece(side_col, side_row), picked.at[2, chip])
-    own_g = local(2, grads.at[0, :, pl.ds(pl.multiple_of(y * PIECE, PIECE), PIECE)], own_grads)
-
-    @pl.when(core == 0)
-    def _():
-        pltpu.make_async_copy(outgrads, mine, local_sems.at[3]).start()
-
-    @pl.when(core == 1)
-    def _():
-        pltpu.make_async_copy(tokens, mine, local_sems.at[3]).start()
+        return slot_quarter.at[row, :, pl.ds(pl.multiple_of(col * PIECE, PIECE), PIECE)]
 
     barrier = pltpu.get_barrier_semaphore()
     for off in offsets:
         back = {k: -v for k, v in off.items()}
         pl.semaphore_signal(barrier, inc=1, device_id=device(**back), device_id_type=MESH)
+    own_p = local(4, pattern_in, pattern)
+    own_o = local(5, owners_in, owners)
+    own_s = local(6, slot.at[:, pl.ds(pl.multiple_of(y * ROWS, ROWS), ROWS)], slot_quarter)
+    own_g = local(2, grads.at[0, :, pl.ds(pl.multiple_of(y * PIECE, PIECE), PIECE)], own_grads)
+
+    @pl.when(core == 0)
+    def _():
+        pltpu.make_async_copy(outgrads, mine, local_sems.at[3]).start()
+
+    @pl.when(core == 1)
+    def _():
+        pltpu.make_async_copy(tokens, mine, local_sems.at[3]).start()
+
     pl.semaphore_wait(barrier, len(offsets))
 
+    def send_quarters(block):
+        sent = []
+        for j, dy in enumerate((1, 3, 2)):
+            ty = wrapped("y", y, dy, 4)
+            src = grads.at[0, block, pl.ds(pl.multiple_of(ty * PIECE, PIECE), PIECE)]
+            sent.append(go(remote(src, grad_in.at[j, block], device(dy=dy))))
+        return sent
+
+    quarters = [send_quarters(0)]
+
+    own_s.wait()
+    own_a = local(0, piece(side_row, side_col), picked.at[0, chip])
+    own_b = local(1, piece(side_col, side_row), picked.at[2, chip])
     scatter = []
     for dx, dz in plane:
         tx = wrapped("x", x, dx, 4)
@@ -140,16 +154,6 @@
         target = device(dx=dx, dz=dz)
         scatter.append(go(remote(piece(row, col), picked.at[0, chip], target)))
         scatter.append(go(remote(piece(col, row), picked.at[2, chip], target)))
-
-    def send_quarters(block):
-        sent = []
-        for j, dy in enumerate((1, 3, 2)):
-            ty = wrapped("y", y, dy, 4)
-            src = grads.at[0, block, pl.ds(pl.multiple_of(ty * PIECE, PIECE), PIECE)]
-            sent.append(go(remote(src, grad_in.at[j, block], device(dy=dy))))
-        return sent
-
-    quarters = [send_quarters(0)]
 
     for copy in (own_p, own_o, own_a, own_b):
         copy.wait()
@@ -281,6 +285,19 @@
     project(-1, 1)
     partial_sum(1)
 
+    own_rows = pl.ds(pl.multiple_of(y * PIECE, PIECE), PIECE)
+    whole = []
+
+    def whole_sum(block):
+        z_parts[block].wait_recv()
+        total = part_out[block].astype(jnp.float32) + part_in[block].astype(jnp.float32)
+        summed[block, own_rows] = total.astype(jnp.bfloat16)
+        ref = summed.at[block, own_rows]
+        whole.extend([go(remote(ref, ref, device(dy=dy))) for dy in (1, 3, 2)])
+
+    early = [copy for copy in pending if all(copy is not part for part in z_parts)]
+    pending[:] = list(z_parts)
+    whole_sum(0)
     for copies in far_cols.values():
         for copy in copies:
             copy.wait_recv()
@@ -289,14 +306,10 @@
     eig_x[x] = eig[...]
     over_x = [go(remote(eig, eig_x.at[x], device(dx=dx))) for dx in (1, 3, 2)]
 
-    own_rows = pl.ds(pl.multiple_of(y * PIECE, PIECE), PIECE)
-    whole = []
-    for block in range(2):
-        z_parts[block].wait_recv()
-        total = part_out[block].astype(jnp.float32) + part_in[block].astype(jnp.float32)
-        summed[block, own_rows] = total.astype(jnp.bfloat16)
-        ref = summed.at[block, own_rows]
-        whole += [go(remote(ref, ref, device(dy=dy))) for dy in (1, 3, 2)]
+    whole_sum(1)
+
+    for copy in early:
+        copy.wait_send()
 
     out_place = z_lo * 2 + lax.div(x, 2)
     in_place = lax.rem(x, 2) * 4
@@ -388,7 +401,7 @@
     def body(*refs):
         kernel(float(token_total), *refs)
 
-    operands = (pattern, owners, tokens, outgrads, grad_parts, basis_slots.reshape(BS, BS))
+    operands = (pattern, owners, tokens, outgrads, grad_parts, basis_slots.reshape(RING, PIECE, BS))
     return pl.pallas_call(
         body,
         out_shape=(jax.ShapeDtypeStruct((2, BS, BS), bf16), jax.ShapeDtypeStruct((2 * NB, BS), f32)),
@@ -397,6 +410,7 @@
         scratch_shapes=[
             pltpu.SMEM((2, NB), jnp.int32),
             pltpu.SMEM((2 * NB,), jnp.int32),
+            pltpu.VMEM((RING, ROWS, BS), bf16),
             pltpu.VMEM((2 * here, NB * BS), bf16),
             pltpu.VMEM((NB + 2, RING, RING, RING, ROWS, PIECE), bf16),
             pltpu.VMEM((3, 16, ROWS, PIECE), bf16),
@@ -413,7 +427,7 @@
             pltpu.VMEM((2, NB, BS), f32),
             pltpu.SemaphoreType.DMA((N_SEMS,)),
             pltpu.SemaphoreType.DMA((N_SEMS,)),
-            pltpu.SemaphoreType.DMA((6,)),
+            pltpu.SemaphoreType.DMA((7,)),
         ],
         compiler_params=pltpu.CompilerParams(
             collective_id=0, has_side_effects=True, vmem_limit_bytes=48 * 2 ** 20),

time: 74.3 us -> 69.9 us (0.941)
  Pallas kernels: 72 us -> 67.6 us
    pallas_call x1, Pallas kernels: 72 us -> 67.6 us  [local(): pl.pallas_call(body, out_shape=(jax.ShapeDtypeStruct((2, BS, BS), bf16),...]
where the time goes in v3:
time: 69.9 us; the launch traced here: 69.8 us
  Pallas kernels  67.6 us (97%)
  local copies, waits for them, and re-layouts  1.59 us (2%)
    pallas_call x1, Pallas kernels, local(): pl.pallas_call(body, out_shape=(jax.ShapeDtypeStruct((2, BS, BS), bf16),...  67.6 us
    unnamed x2, local copies, waits for them, and re-layouts  1.59 us

profile of v3, /device:TPU:1, one launch (start us, length us, event | category | flops | bytes accessed | tf_op | source)
XLA Modules:
  0.0 69.8 jit_solution(7066312325716250353)
XLA Ops:
  0.6 67.6 %shard_map.77 = (bf16[2,512,512]{2,1,0:T(8,128)(2,1)S(1)}, f32[16,512]{1,0:T(8,128)S(1)}) custom-call(s32[2,8]{1,0:T(2,128)} %refs_0_.1, s32[16]{0:T(128)} %refs_1_.1, bf16[512,4096]{1,0:T(8,128)(2,1)} %refs_2_.1, bf16[512,4096]{1,0:T(8,128)(2,1)} %refs_3_.1, bf16[1,2,512,512]{3,2,1,0:T(8,128)(2,1)} %refs_4_.1, bf16[4,128,512]{2,1,0:T(8,128)(2,1)} %bitcast.1), custom_call_target="tpu_custom_call" | custom-call | tf_op jit(solution)/shard_map/pallas_call | solution.py:405
  68.2 1.0 %copy.10 = bf16[2,512,512]{2,1,0:T(8,128)(2,1)} copy(bf16[2,512,512]{2,1,0:T(8,128)(2,1)S(1)} %get-tuple-element.4) | data formatting | bytes 2097152
  69.2 0.6 copy.11

commit v4 on v3

--- a/solution.py
+++ b/solution.py
@@ -279,11 +279,10 @@
             eig[:, columns] = sums[:, n * PIECE:(n + 1) * PIECE]
 
     pass_on(-1, rest)
-    project(0)
     pass_on(1, rest)
     pass_on(2, rest)
+    partial_sum(1)
     project(-1, 1)
-    partial_sum(1)
 
     own_rows = pl.ds(pl.multiple_of(y * PIECE, PIECE), PIECE)
     whole = []
@@ -301,15 +300,10 @@
     for copies in far_cols.values():
         for copy in copies:
             copy.wait_recv()
-    project(2)
+    project(0, 2)
 
     eig_x[x] = eig[...]
     over_x = [go(remote(eig, eig_x.at[x], device(dx=dx))) for dx in (1, 3, 2)]
-
-    whole_sum(1)
-
-    for copy in early:
-        copy.wait_send()
 
     out_place = z_lo * 2 + lax.div(x, 2)
     in_place = lax.rem(x, 2) * 4
@@ -324,10 +318,13 @@
     def _():
         two_bases.start()
 
+    for copy in early:
+        copy.wait_send()
     for copy in over_x:
         copy.wait_recv()
     eig_y[y] = (eig_x[0] + eig_x[1]) + (eig_x[2] + eig_x[3])
     over_y = [go(remote(eig_y.at[y], eig_y.at[y], device(dy=dy))) for dy in (1, 3, 2)]
+    whole_sum(1)
 
     @pl.when(core == 0)
     def _():
@@ -339,29 +336,28 @@
         one_basis.wait_recv()
         two_bases.wait_send()
 
+    out_basis = out_place * (1 - core) + NB * core
+
+    def in_basis(j):
+        return (NB + j) * (1 - core) + (in_place + 2 + j) * core
+
+    def basis(place):
+        return jnp.concatenate([columns_of(place, col) for col in range(RING)], axis=1)
+
+    def rotate(j):
+        for copy in whole[3 * j:3 * j + 3]:
+            copy.wait_recv()
+        halfway = lax.dot_general(basis(out_basis), summed[j], (((0,), (0,)), ((), ())),
+                                  preferred_element_type=jnp.float32).astype(jnp.bfloat16)
+        rotated[j] = jnp.dot(halfway, basis(in_basis(j)), preferred_element_type=jnp.float32)
+
+    rotate(0)
     for copy in over_y:
         copy.wait_recv()
     eig_z[z] = (eig_y[0] + eig_y[1]) + (eig_y[2] + eig_y[3])
     over_z = [go(remote(eig_z.at[z], eig_z.at[z], device(dz=dz))) for dz in (1, -1, 2, -2, 3, -3, 4)]
 
-    out_basis = out_place * (1 - core) + NB * core
-
-    def in_basis(j):
-        return (NB + j) * (1 - core) + (in_place + 2 + j) * core
-
-    def basis(place):
-        return jnp.concatenate([columns_of(place, col) for col in range(RING)], axis=1)
-
-    for copy in whole:
-        copy.wait_recv()
-
-    def rotate(j, _):
-        halfway = lax.dot_general(basis(out_basis), summed[j], (((0,), (0,)), ((), ())),
-                                  preferred_element_type=jnp.float32).astype(jnp.bfloat16)
-        rotated[j] = jnp.dot(halfway, basis(in_basis(j)), preferred_element_type=jnp.float32)
-        return 0
-
-    lax.fori_loop(0, 2, rotate, 0)
+    rotate(1)
     flush_later = list(pending)
     pending.clear()
     for copy in over_z:

time: 69.9 us -> 67.9 us (0.971)
  Pallas kernels: 67.6 us -> 65.6 us
    pallas_call x1, Pallas kernels: 67.6 us -> 65.6 us  [local(): pl.pallas_call(body, out_shape=(jax.ShapeDtypeStruct((2, BS, BS), bf16),...]
where the time goes in v4:
time: 67.9 us; the launch traced here: 67.8 us
  Pallas kernels  65.6 us (97%)
  local copies, waits for them, and re-layouts  1.59 us (2%)
    pallas_call x1, Pallas kernels, local(): pl.pallas_call(body, out_shape=(jax.ShapeDtypeStruct((2, BS, BS), bf16),...  65.6 us
    unnamed x2, local copies, waits for them, and re-layouts  1.59 us

profile of v4, /device:TPU:1, one launch (start us, length us, event | category | flops | bytes accessed | tf_op | source)
XLA Modules:
  0.0 67.8 jit_solution(7613618861997273913)
XLA Ops:
  0.6 65.6 %shard_map.77 = (bf16[2,512,512]{2,1,0:T(8,128)(2,1)S(1)}, f32[16,512]{1,0:T(8,128)S(1)}) custom-call(s32[2,8]{1,0:T(2,128)} %refs_0_.1, s32[16]{0:T(128)} %refs_1_.1, bf16[512,4096]{1,0:T(8,128)(2,1)} %refs_2_.1, bf16[512,4096]{1,0:T(8,128)(2,1)} %refs_3_.1, bf16[1,2,512,512]{3,2,1,0:T(8,128)(2,1)} %refs_4_.1, bf16[4,128,512]{2,1,0:T(8,128)(2,1)} %bitcast.1), custom_call_target="tpu_custom_call" | custom-call | tf_op jit(solution)/shard_map/pallas_call | solution.py:401
  66.2 1.0 %copy.10 = bf16[2,512,512]{2,1,0:T(8,128)(2,1)} copy(bf16[2,512,512]{2,1,0:T(8,128)(2,1)S(1)} %get-tuple-element.4) | data formatting | bytes 2097152
  67.2 0.6 copy.11

commit v5 on v4

--- a/solution.py
+++ b/solution.py
@@ -303,7 +303,7 @@
     project(0, 2)
 
     eig_x[x] = eig[...]
-    over_x = [go(remote(eig, eig_x.at[x], device(dx=dx))) for dx in (1, 3, 2)]
+    over_x = [go(remote(eig, eig_x.at[x], device(dx=dx))) for dx in (2, 1, 3)]
 
     out_place = z_lo * 2 + lax.div(x, 2)
     in_place = lax.rem(x, 2) * 4
@@ -323,7 +323,7 @@
     for copy in over_x:
         copy.wait_recv()
     eig_y[y] = (eig_x[0] + eig_x[1]) + (eig_x[2] + eig_x[3])
-    over_y = [go(remote(eig_y.at[y], eig_y.at[y], device(dy=dy))) for dy in (1, 3, 2)]
+    over_y = [go(remote(eig_y.at[y], eig_y.at[y], device(dy=dy))) for dy in (2, 1, 3)]
     whole_sum(1)
 
     @pl.when(core == 0)
@@ -355,7 +355,7 @@
     for copy in over_y:
         copy.wait_recv()
     eig_z[z] = (eig_y[0] + eig_y[1]) + (eig_y[2] + eig_y[3])
-    over_z = [go(remote(eig_z.at[z], eig_z.at[z], device(dz=dz))) for dz in (1, -1, 2, -2, 3, -3, 4)]
+    over_z = [go(remote(eig_z.at[z], eig_z.at[z], device(dz=dz))) for dz in (4, 3, -3, 2, -2, 1, -1)]
 
     rotate(1)
     flush_later = list(pending)

time: 67.9 us -> 67.3 us (level)
  no operation moved by 1% of the time
where the time goes in v5:
time: 67.3 us; the launch traced here: 67.2 us
  Pallas kernels  65 us (97%)
  local copies, waits for them, and re-layouts  1.59 us (2%)
    pallas_call x1, Pallas kernels, local(): pl.pallas_call(body, out_shape=(jax.ShapeDtypeStruct((2, BS, BS), bf16),...  65 us
    unnamed x2, local copies, waits for them, and re-layouts  1.59 us

profile of v5, /device:TPU:1, one launch (start us, length us, event | category | flops | bytes accessed | tf_op | source)
XLA Modules:
  0.0 67.2 jit_solution(7929436602024235865)
XLA Ops:
  0.6 65.0 %shard_map.77 = (bf16[2,512,512]{2,1,0:T(8,128)(2,1)S(1)}, f32[16,512]{1,0:T(8,128)S(1)}) custom-call(s32[2,8]{1,0:T(2,128)} %refs_0_.1, s32[16]{0:T(128)} %refs_1_.1, bf16[512,4096]{1,0:T(8,128)(2,1)} %refs_2_.1, bf16[512,4096]{1,0:T(8,128)(2,1)} %refs_3_.1, bf16[1,2,512,512]{3,2,1,0:T(8,128)(2,1)} %refs_4_.1, bf16[4,128,512]{2,1,0:T(8,128)(2,1)} %bitcast.1), custom_call_target="tpu_custom_call" | custom-call | tf_op jit(solution)/shard_map/pallas_call | solution.py:401
  65.7 1.0 %copy.10 = bf16[2,512,512]{2,1,0:T(8,128)(2,1)} copy(bf16[2,512,512]{2,1,0:T(8,128)(2,1)S(1)} %get-tuple-element.4) | data formatting | bytes 2097152
  66.6 0.6 copy.11
